TPU v7x, 32 devices: a whole 2x2x4 slice. The times are simulated.
32 devices in a mesh: prod: 8 (over y, x, core), pre: 4 (over z).
Axes of the slice: x: 2, y: 2, z: 4, core: 2. Of those that a mesh axis runs over, the one named last changes fastest.
Arguments:
- potentials: bfloat16 [128, 16, 512], P(('prod', 'pre')), may hold values from -6 to 6
- injected: float32 [128, 16, 512], P(('prod', 'pre')), may hold values from -6 to 6
- near_blocks: bfloat16 [128, 4, 512, 512], P('prod', 'pre'), may hold values from -0.125 to 0.125
- near_cols: int32 [128, 4], P('prod', 'pre'), may hold values from 0 to 127, as said below
- row_basis: bfloat16 [128, 16, 512], P('prod'), may hold values from -1.5 to 1.5
- col_basis: bfloat16 [128, 16, 512], P(('prod', 'pre')), may hold values from -0.25 to 0.25
- basis_ranks: int32 [128], P(('prod', 'pre')), may hold values from 1 to 16
- couplings: bfloat16 [128, 16, 2048], P('prod', None, 'pre'), may hold values from -0.125 to 0.125
- inverses: bfloat16 [128, 512, 512], P(('prod', 'pre')), may hold values from -0.25 to 0.25
Outputs:
- residual: float32 [128, 16, 512], P(('prod', 'pre'))
- corrected: float32 [128, 16, 512], P(('prod', 'pre'))
Inputs may be any that keep to these rules, and one draw needn't show every extreme that they name: near_cols[i, 0] = i; near_cols[i, 1] is i + 8 or i - 8; every other entry differs from i by 1 to 7.
All inputs are finite; a program needn't handle non-finite values.
Results may differ from a plain program's by a relative error of at most 0.012.
Values may be sent and summed in bfloat16 or wider, within the bound.
A program may use at most 64 MiB of HBM per device.

v0:
```python
import jax
import jax.numpy as jnp
from jax import lax
from jax.sharding import PartitionSpec as P


def with_halo(block, sides, width):
    for axis, dim in sides:
        count = lax.axis_size(axis)
        forward = [(i, i + 1) for i in range(count - 1)]
        backward = [(target, source) for source, target in forward]
        low = lax.ppermute(
            lax.slice_in_dim(block, block.shape[dim] - width, None, axis=dim), axis, forward
        )
        high = lax.ppermute(lax.slice_in_dim(block, 0, width, axis=dim), axis, backward)
        block = jnp.concatenate([low, block, high], axis=dim)
    return block


def local(
    potentials,
    injected,
    near_blocks,
    near_cols,
    row_basis,
    col_basis,
    basis_ranks,
    couplings,
    inverses,
):
    rows_here = near_blocks.shape[0]
    owned_count = potentials.shape[0]
    scenarios = potentials.shape[1]
    rank_cap = col_basis.shape[1]
    band_width = rows_here // 2
    coeffs = lax.dot_general(
        potentials, col_basis, (((2,), (2,)), ((0,), (0,))), preferred_element_type=jnp.float32
    )
    levels = lax.broadcasted_iota(jnp.int32, (owned_count, rank_cap), 1)
    kept_levels = levels < basis_ranks[:, None]
    coeffs = jnp.where(kept_levels[:, None, :], coeffs, jnp.zeros_like(coeffs)).astype(jnp.bfloat16)
    coeffs = jnp.transpose(coeffs, (1, 0, 2)).reshape(scenarios, owned_count * rank_cap)
    column_coeffs = lax.all_gather(coeffs, "prod", axis=1, tiled=True)
    flat_couplings = couplings.reshape(rows_here * rank_cap, couplings.shape[2])
    weights = lax.dot_general(
        flat_couplings, column_coeffs, (((1,), (1,)), ((), ())), preferred_element_type=jnp.float32
    )
    weights = weights.reshape(rows_here, rank_cap, scenarios).astype(jnp.bfloat16)
    grouped = lax.all_gather(potentials, "pre", axis=0, tiled=True)
    banded = with_halo(grouped, (("prod", 0),), band_width)
    offset = lax.axis_index("prod") * rows_here - band_width
    local_index = near_cols - offset
    picked = banded[local_index]
    near_part = lax.dot_general(
        picked, near_blocks, (((1, 3), (1, 3)), ((0,), (0,))), preferred_element_type=jnp.float32
    )
    far_part = lax.dot_general(
        weights, row_basis, (((1,), (1,)), ((0,), (0,))), preferred_element_type=jnp.float32
    )
    partial_value = near_part + far_part
    summed = lax.psum_scatter(
        partial_value.astype(jnp.bfloat16), "pre", scatter_dimension=0, tiled=True
    ).astype(jnp.float32)
    residual = injected - summed
    halfway = residual.astype(jnp.bfloat16)
    corrected = lax.dot_general(
        halfway, inverses, (((2,), (2,)), ((0,), (0,))), preferred_element_type=jnp.float32
    )
    return (residual, corrected)


def solution(mesh):
    return jax.shard_map(
        local,
        mesh=mesh,
        in_specs=(
            P(("prod", "pre"), None, None),
            P(("prod", "pre"), None, None),
            P("prod", "pre", None, None),
            P("prod", "pre"),
            P("prod", None, None),
            P(("prod", "pre"), None, None),
            P(("prod", "pre")),
            P("prod", None, "pre"),
            P(("prod", "pre"), None, None),
        ),
        out_specs=(P(("prod", "pre"), None, None), P(("prod", "pre"), None, None)),
        check_vma=False,
    )
```

profile of v0, /device:TPU:0, one launch (start us, length us, event | category | flops | bytes accessed | tf_op | source)
XLA Modules:
  0.0 81.3 jit_solution(9527547756558137753)
XLA Ops:
  7.2 0.0 copy-start
  7.2 0.0 copy-start.2
  7.2 0.0 reduce-scatter.2.cloned.1.call-start
  7.2 16.0 %all_gather.6 = bf16[16,16,512]{2,1,0:T(8,128)(2,1)S(1)} all-gather(bf16[4,16,512]{2,1,0:T(8,128)(2,1)} %param.9), channel_id=1, replica_groups=mesh['prod'=8,'pre'=4] {'pre'}, dimensions={0}, use_global_device_ids=true | all-gather | bytes 327680 | tf_op jit(solution)/shard_map/all_gather | solution.py:49
  23.2 1.9 %collective-permute-start = (bf16[8,16,512]{2,1,0:T(8,128)(2,1)S(1)}, bf16[8,16,512]{2,1,0:T(8,128)(2,1)}, u32[]{:S(2)}, u32[]{:S(2)}) collective-permute-start(bf16[8,16,512]{2,1,0:T(8,128)(2,1)S(1)} %get-tuple-element.2), channel_id=1, source_target_pairs={{0,4},{4,8},{8,12},{12,16},{16,20},{20,24},{24,28},{1,5},{5,9},{9,... | collective-permute-start | bytes 393224 | tf_op jit(solution)/shard_map/ppermute | solution.py:12
  25.2 1.3 %collective-permute-start.1 = (bf16[8,16,512]{2,1,0:T(8,128)(2,1)S(1)}, bf16[8,16,512]{2,1,0:T(8,128)(2,1)}, u32[]{:S(2)}, u32[]{:S(2)}) collective-permute-start(bf16[8,16,512]{2,1,0:T(8,128)(2,1)S(1)} %get-tuple-element.3), channel_id=1, source_target_pairs={{4,0},{8,4},{12,8},{16,12},{20,16},{24,20},{28,24},{5,1},{9,5},{13... | collective-permute-start | bytes 393224 | tf_op jit(solution)/shard_map/ppermute | solution.py:15
  26.5 0.7 iota_compare_fusion
  27.2 1.0 %fusion.9 = bf16[16,4,16]{2,0,1:T(8,128)(2,1)S(1)} fusion(bf16[4,16,512]{2,1,0:T(8,128)(2,1)} %param.9, bf16[4,16,512]{2,1,0:T(8,128)(2,1)} %param.14, pred[4,16]{1,0:T(4,128)(4,1)S(1)} %iota_compare_fusion), kind=kOutput, calls=%fused_computation.7 | convolution fusion | flops 1050624 | bytes 133184 | tf_op jit(solution)/shard_map/dot_general | solution.py:36
  28.2 0.1 reshape.35
  28.3 12.3 %all-gather = bf16[8,64,16]{1,2,0:T(8,128)(2,1)S(1)} all-gather(bf16[1,64,16]{1,2,0:T(8,128)(2,1)S(1)} %bitcast.29), channel_id=1, replica_groups=mesh['prod'=8,'pre'=4] {'prod'}, dimensions={0}, use_global_device_ids=true | all-gather | bytes 18432 | tf_op jit(solution)/shard_map/all_gather | solution.py:43
  40.6 0.1 reshape.48
  40.7 1.1 %fusion.10 = bf16[256,16]{0,1:T(8,128)(2,1)S(1)} fusion(bf16[512,16]{0,1:T(8,128)(2,1)S(1)} %reshape.48, bf16[256,512]{1,0:T(8,128)(2,1)} %bitcast.28), kind=kOutput, calls=%fused_computation.9 | convolution fusion | flops 4198400 | bytes 286720 | tf_op jit(solution)/shard_map/dot_general | solution.py:45
  41.8 0.1 convert_element_type.29
  42.0 1.1 %fusion.11 = f32[16,16,512]{2,1,0:T(8,128)S(1)} fusion(bf16[16,16,512]{2,1,0:T(8,128)(2,1)} %param.13, bf16[16,16,16]{1,0,2:T(8,128)(2,1)S(1)} %convert_element_type.29), kind=kOutput, calls=%fused_computation.12 | convolution fusion | flops 4194304 | bytes 794624 | tf_op jit(solution)/shard_map/dot_general | solution.py:57
  43.1 0.7 fusion.15
  43.8 0.0 collective-permute-done
  43.8 0.0 collective-permute-done.1
  43.8 1.0 %pad_maximum_fusion = bf16[32,16,512]{2,1,0:T(8,128)(2,1)S(1)} fusion(bf16[8,16,512]{2,1,0:T(8,128)(2,1)} %collective-permute-done.1, bf16[16,16,512]{2,1,0:T(8,128)(2,1)S(1)} %all_gather.6, bf16[8,16,512]{2,1,0:T(8,128)(2,1)} %collective-permute-done), kind=kLoop, calls=%fused_computation.10 | loop fusion | flops 524288 | bytes 1048576 | tf_op jit(solution)/shard_map/concatenate | solution.py:16
  44.9 0.6 gather_fusion
  45.4 6.4 %fusion.5 = bf16[16,16,512]{2,1,0:T(8,128)(2,1)} fusion(f32[16,16,512]{2,1,0:T(8,128)S(1)} %fusion.11, bf16[16,16,512]{2,1,0:T(8,128)(2,1)S(1)} %gather_fusion, bf16[16,1,512,512]{3,2,1,0:T(8,128)(2,1)} %param.11), kind=kOutput, calls=%fused_computation.4 | convolution fusion | flops 134479872 | bytes 9437184 | tf_op jit(solution)/shard_map/dot_general | solution.py:54
  51.8 0.0 reduce-scatter.2.cloned.1.call-update
  51.8 20.4 %reduce-scatter.2.cloned.1.call-done = bf16[4,16,512]{2,1,0:T(8,128)(2,1)} async-done(((bf16[16,16,512]{2,1,0:T(8,128)(2,1)}), bf16[4,16,512]{2,1,0:T(8,128)(2,1)}) %reduce-scatter.2.cloned.1.call-update) | async-done | bytes 65552 | tf_op jit(solution)/shard_map/reduce_scatter | solution.py:61
  72.2 0.0 copy-done.2
  72.2 0.9 %convert_subtract_fusion = f32[4,16,512]{2,1,0:T(8,128)S(1)} fusion(f32[4,16,512]{2,1,0:T(8,128)S(1)} %copy-done.2, bf16[4,16,512]{2,1,0:T(8,128)(2,1)} %reduce-scatter.2.cloned.1.call-done), kind=kLoop, calls=%fused_computation.11 | loop fusion | flops 65536 | bytes 327680 | tf_op jit(solution)/shard_map/sub | solution.py:64
  73.1 0.0 copy-done
  73.1 0.0 copy-start.1
  73.1 1.3 %fusion.13 = f32[4,16,512]{2,1,0:T(8,128)} fusion(bf16[4,512,512]{2,1,0:T(8,128)(2,1)S(1)} %copy-done, f32[4,16,512]{2,1,0:T(8,128)S(1)} %convert_subtract_fusion), kind=kOutput, calls=%fused_computation.14 | convolution fusion | flops 33587200 | bytes 2359296 | tf_op jit(solution)/shard_map/dot_general | solution.py:66
  74.4 0.0 copy-done.1
  (4 shorter events, 0.1 us)
Async XLA Ops:
  7.2 65.9 %copy-start = (bf16[4,512,512]{2,1,0:T(8,128)(2,1)S(1)}, bf16[4,512,512]{2,1,0:T(8,128)(2,1)}, u32[]{:S(2)}) copy-start(bf16[4,512,512]{2,1,0:T(8,128)(2,1)} %param.17) | copy-start | bytes 6291460
  7.2 65.0 %copy-start.2 = (f32[4,16,512]{2,1,0:T(8,128)S(1)}, f32[4,16,512]{2,1,0:T(8,128)}, u32[]{:S(2)}) copy-start(f32[4,16,512]{2,1,0:T(8,128)} %param.10) | copy-start | bytes 393220
  7.2 65.0 %reduce-scatter.2.cloned.1.call-start = ((), (), s32[]{:S(2)}) async-start(), calls=%async_computation.1 | async-start | bytes 327680 | tf_op jit(solution)/shard_map/reduce_scatter | solution.py:61
  23.2 20.6 %collective-permute-start = (bf16[8,16,512]{2,1,0:T(8,128)(2,1)S(1)}, bf16[8,16,512]{2,1,0:T(8,128)(2,1)}, u32[]{:S(2)}, u32[]{:S(2)}) collective-permute-start(bf16[8,16,512]{2,1,0:T(8,128)(2,1)S(1)} %get-tuple-element.2), channel_id=1, source_target_pairs={{0,4},{4,8},{8,12},{12,16},{16,20},{20,24},{24,28},{1,5},{5,9},{9,... | collective-permute-start | bytes 393224 | tf_op jit(solution)/shard_map/ppermute | solution.py:12
  25.2 18.6 %collective-permute-start.1 = (bf16[8,16,512]{2,1,0:T(8,128)(2,1)S(1)}, bf16[8,16,512]{2,1,0:T(8,128)(2,1)}, u32[]{:S(2)}, u32[]{:S(2)}) collective-permute-start(bf16[8,16,512]{2,1,0:T(8,128)(2,1)S(1)} %get-tuple-element.3), channel_id=1, source_target_pairs={{4,0},{8,4},{12,8},{16,12},{20,16},{24,20},{28,24},{5,1},{9,5},{13... | collective-permute-start | bytes 393224 | tf_op jit(solution)/shard_map/ppermute | solution.py:15
  73.1 1.3 %copy-start.1 = (f32[4,16,512]{2,1,0:T(8,128)}, f32[4,16,512]{2,1,0:T(8,128)S(1)}, u32[]{:S(2)}) copy-start(f32[4,16,512]{2,1,0:T(8,128)S(1)} %convert_subtract_fusion) | copy-start | bytes 393220
Sparse Core Ops, SparseCore 0:
  52.0 20.1 reduce-scatter.1
where the time goes:
time: 81.7 us; the launch traced here: 81.3 us
  blocking collectives  28.3 us (35%)
  waiting for transfers between devices  20.4 us (25%)
  between operations  14.1 us (17%)
  matrix products  10.9 us (13%)
  other arithmetic  3.29 us (4%)
  starting transfers between devices  3.27 us (4%)
  local copies, waits for them, and re-layouts  0.96 us (1%)
    reduce_scatter x1, waiting for transfers between devices, local(): lax.psum_scatter(partial_value.astype(jnp.bfloat16), 'pre', scatter_dimen...  20.4 us
    all_gather x1, blocking collectives, local(): grouped = lax.all_gather(potentials, 'pre', axis=0, tiled=True)  16 us
    all_gather x1, blocking collectives, local(): column_coeffs = lax.all_gather(coeffs, 'prod', axis=1, tiled=True)  12.3 us
    dot_general x1, matrix products, local(): lax.dot_general(picked, near_blocks, (((1, 3), (1, 3)), ((0,), (0,))), pr...  6.38 us
    ppermute x1, starting transfers between devices, with_halo(): lax.ppermute(lax.slice_in_dim(block, block.shape[dim] - width, None, axis...  1.95 us
  transfers between devices with their start and end apart: 3, of which 1 were waited for; matrix products, arithmetic and copies ran while one was open for 6% of the time, Pallas kernels for 0%

commit v1 on v0

v1 whole, which is shorter than its diff:
```python
import functools

import jax
import jax.numpy as jnp
from jax import lax
from jax.experimental import pallas as pl
from jax.experimental.pallas import tpu as pltpu
from jax.sharding import PartitionSpec as P

MESH = pl.DeviceIdType.MESH
NT = (((1,), (1,)), ((), ()))


def kernel(
    n_prod,
    n_pre,
    pot_hbm,
    inj_hbm,
    near_hbm,
    cols_ref,
    rowb_hbm,
    colb_hbm,
    ranks_ref,
    coup_hbm,
    inv_hbm,
    res_ref,
    cor_ref,
    band,
    inj,
    near,
    rowb,
    colb,
    coup,
    inv,
    coef,
    far,
    mine,
    sending,
    arriving,
    load_sem,
    near_sem,
    gather_send,
    gather_recv,
    halo_send,
    halo_recv,
    coef_send,
    coef_recv,
    part_send,
    part_recv,
):
    owned, scen, panels = pot_hbm.shape
    rows = near_hbm.shape[0]
    rank_cap = colb_hbm.shape[1]
    half_rows = rows // 2
    half = n_pre // 2
    width = owned * rank_cap
    p = lax.axis_index("prod")
    z = lax.axis_index("pre")
    high, low = z // half, z % half
    others = [(1 - high) * half + (low + e) % half for e in range(half)]
    others += [high * half + (low + e) % half for e in range(1, half)]
    nearest = others[half:] + others[:half]

    def slot(first):
        return band.at[pl.ds(first, owned)]

    own = half_rows + z * owned
    load_pot = pltpu.make_async_copy(pot_hbm, slot(own), load_sem.at[0])
    load_colb = pltpu.make_async_copy(colb_hbm, colb, load_sem.at[1])
    load_coup = pltpu.make_async_copy(coup_hbm, coup, load_sem.at[2])
    load_rowb = pltpu.make_async_copy(rowb_hbm, rowb, load_sem.at[3])
    load_inj = pltpu.make_async_copy(inj_hbm, inj, load_sem.at[4])
    load_inv = pltpu.make_async_copy(inv_hbm, inv, load_sem.at[5])
    load_pot.start()
    load_colb.start()

    barrier = pltpu.get_barrier_semaphore()
    for target in others:
        pl.semaphore_signal(barrier, inc=1, device_id=(p, target), device_id_type=MESH)
    for e in range(1, n_prod):
        pl.semaphore_signal(
            barrier, inc=1, device_id=((p + e) % n_prod, z), device_id_type=MESH
        )
    load_coup.start()
    load_rowb.start()
    near_loads = []
    for step, target in enumerate(others + [z]):
        near_loads.append(
            pltpu.make_async_copy(
                near_hbm.at[pl.ds(target * owned, owned), 0],
                near.at[pl.ds(target * owned, owned)],
                near_sem.at[step],
            )
        )
        near_loads[-1].start()
    load_inj.start()
    load_inv.start()
    load_pot.wait()
    load_colb.wait()
    pl.semaphore_wait(barrier, n_pre - 1 + n_prod - 1)

    gathers = []
    for e, target in enumerate(others):
        gathers.append(
            pltpu.make_async_remote_copy(
                src_ref=slot(own),
                dst_ref=slot(own),
                send_sem=gather_send.at[e],
                recv_sem=gather_recv.at[z],
                device_id=(p, target),
                device_id_type=MESH,
            )
        )
        gathers[-1].start()

    halos = []

    def forward(zs, index):
        lower = zs < half
        to = jnp.where(lower, p - 1, p + 1)
        first = half_rows + zs * owned
        there = jnp.where(lower, first + rows, first - rows)
        ok = (z >= 1) & (to >= 0) & (to < n_prod)
        copy = pltpu.make_async_remote_copy(
            src_ref=slot(first),
            dst_ref=slot(there),
            send_sem=halo_send.at[index],
            recv_sem=halo_recv.at[zs],
            device_id=(to, z),
            device_id_type=MESH,
        )

        @pl.when(ok)
        def _():
            copy.start()

        halos.append((ok, copy))

    forward(z, 0)

    pot = band[pl.ds(own, owned)].reshape(owned * scen, panels)
    basis = colb[...].reshape(width, panels)
    products = lax.dot_general(
        pot,
        jnp.concatenate([basis] * (128 // width), axis=0),
        NT,
        preferred_element_type=jnp.float32,
    )
    lane = lax.broadcasted_iota(jnp.int32, (scen, 128), 1)
    inner = lane % width
    here = (lane // width) == p % (128 // width)
    mine_coef = jnp.zeros((scen, 128), jnp.float32)
    for j in range(owned):
        keep = here & (inner // rank_cap == j) & (inner % rank_cap < ranks_ref[j])
        mine_coef = jnp.where(keep, products[j * scen : (j + 1) * scen], mine_coef)
    coef[p] = mine_coef.astype(jnp.bfloat16)
    coef_copies = []
    for e in range(1, n_prod):
        coef_copies.append(
            pltpu.make_async_remote_copy(
                src_ref=coef.at[p],
                dst_ref=coef.at[p],
                send_sem=coef_send.at[e],
                recv_sem=coef_recv.at[p],
                device_id=((p + e) % n_prod, z),
                device_id_type=MESH,
            )
        )
        coef_copies[-1].start()

    for index, zs in enumerate(nearest):
        pltpu.make_async_remote_copy(
            src_ref=slot(half_rows + zs * owned),
            dst_ref=slot(half_rows + zs * owned),
            send_sem=gather_send.at[0],
            recv_sem=gather_recv.at[zs],
            device_id=(p, zs),
            device_id_type=MESH,
        ).wait_recv()
        forward(zs, index + 1)

    for e in range(1, n_prod):
        b = (p + e) % n_prod
        pltpu.make_async_remote_copy(
            src_ref=coef.at[b],
            dst_ref=coef.at[b],
            send_sem=coef_send.at[0],
            recv_sem=coef_recv.at[b],
            device_id=(b, z),
            device_id_type=MESH,
        ).wait_recv()
    load_coup.wait()
    load_rowb.wait()
    share = 128 // width
    blocks = []
    for m in range(n_prod // share):
        block = coef[m * share]
        for e in range(1, share):
            block = block + coef[m * share + e]
        blocks.append(block)
    columns = jnp.concatenate(blocks, axis=1)
    weights = lax.dot_general(
        columns,
        coup[...].reshape(rows * rank_cap, n_prod * width),
        NT,
        preferred_element_type=jnp.float32,
    )
    weights = jnp.concatenate([weights] * rows, axis=0)
    shape = (rows * scen, rows * rank_cap)
    row_of = lax.broadcasted_iota(jnp.int32, shape, 0) // scen
    col_of = lax.broadcasted_iota(jnp.int32, shape, 1) // rank_cap
    weights = jnp.where(row_of == col_of, weights, 0.0).astype(jnp.bfloat16)
    far[...] = jnp.dot(
        weights,
        rowb[...].reshape(rows * rank_cap, panels),
        preferred_element_type=jnp.float32,
    ).reshape(rows, scen, panels)

    for zs in range(n_pre):
        source = p + 1 if zs < half else p - 1
        first = half_rows + zs * owned + (rows if zs < half else -rows)

        @pl.when((z >= 1) & (source >= 0) & (source < n_prod))
        def _():
            pltpu.make_async_remote_copy(
                src_ref=slot(first),
                dst_ref=slot(first),
                send_sem=halo_send.at[0],
                recv_sem=halo_recv.at[zs],
                device_id=(source, z),
                device_id_type=MESH,
            ).wait_recv()

    offset = p * rows - half_rows

    def partial_row(row):
        picked = band[jnp.clip(cols_ref[row] - offset, 0, 2 * rows - 1)]
        value = lax.dot_general(picked, near[row], NT, preferred_element_type=jnp.float32)
        return value + far[row]

    parts = []
    for e, target in enumerate(others):
        near_loads[e].wait()
        for j in range(owned):
            row = target * owned + j
            sending[e, j] = partial_row(row).astype(jnp.bfloat16)
        parts.append(
            pltpu.make_async_remote_copy(
                src_ref=sending.at[e],
                dst_ref=arriving.at[z],
                send_sem=part_send.at[e],
                recv_sem=part_recv.at[z],
                device_id=(p, target),
                device_id_type=MESH,
            )
        )
        parts[-1].start()
    near_loads[-1].wait()
    load_inj.wait()
    for j in range(owned):
        mine[j] = inj[j] - partial_row(z * owned + j)
    load_inv.wait()
    for zs in nearest:
        pltpu.make_async_remote_copy(
            src_ref=arriving.at[zs],
            dst_ref=arriving.at[zs],
            send_sem=part_send.at[0],
            recv_sem=part_recv.at[zs],
            device_id=(p, zs),
            device_id_type=MESH,
        ).wait_recv()
    for j in range(owned):
        summed = arriving[others[0], j].astype(jnp.float32)
        for zs in others[1:]:
            summed = summed + arriving[zs, j].astype(jnp.float32)
        residual = mine[j] - summed
        res_ref[j] = residual
        cor_ref[j] = lax.dot_general(
            residual.astype(jnp.bfloat16), inv[j], NT, preferred_element_type=jnp.float32
        )
    for copy in gathers + coef_copies + parts:
        copy.wait_send()
    for ok, copy in halos:

        @pl.when(ok)
        def _():
            copy.wait_send()


def local(n_prod, n_pre, potentials, injected, near, cols, rowb, colb, ranks, coup, inv):
    owned, scen, panels = potentials.shape
    rows = near.shape[0]
    out = jax.ShapeDtypeStruct(injected.shape, jnp.float32)
    anywhere = pl.BlockSpec(memory_space=pltpu.HBM)
    scalars = pl.BlockSpec(memory_space=pltpu.SMEM)
    vmem = pl.BlockSpec(memory_space=pltpu.VMEM)
    dma = pltpu.SemaphoreType.DMA
    blocks = rows + owned
    return pl.pallas_call(
        functools.partial(kernel, n_prod, n_pre),
        out_shape=(out, out),
        in_specs=[
            anywhere,
            anywhere,
            anywhere,
            scalars,
            anywhere,
            anywhere,
            scalars,
            anywhere,
            anywhere,
        ],
        out_specs=(vmem, vmem),
        scratch_shapes=[
            pltpu.VMEM((2 * rows, scen, panels), jnp.bfloat16),
            pltpu.VMEM(injected.shape, jnp.float32),
            pltpu.VMEM((rows, panels, panels), jnp.bfloat16),
            pltpu.VMEM(rowb.shape, jnp.bfloat16),
            pltpu.VMEM(colb.shape, jnp.bfloat16),
            pltpu.VMEM(coup.shape, jnp.bfloat16),
            pltpu.VMEM(inv.shape, jnp.bfloat16),
            pltpu.VMEM((n_prod, scen, 128), jnp.bfloat16),
            pltpu.VMEM((rows, scen, panels), jnp.float32),
            pltpu.VMEM(injected.shape, jnp.float32),
            pltpu.VMEM((n_pre - 1, owned, scen, panels), jnp.bfloat16),
            pltpu.VMEM((n_pre, owned, scen, panels), jnp.bfloat16),
            dma((6,)),
            dma((n_pre,)),
            dma((n_pre,)),
            dma((n_pre,)),
            dma((n_pre,)),
            dma((n_pre,)),
            dma((n_prod,)),
            dma((n_prod,)),
            dma((n_pre,)),
            dma((n_pre,)),
        ],
        compiler_params=pltpu.CompilerParams(
            collective_id=0, has_side_effects=True, vmem_limit_bytes=63 * 2**20
        ),
        cost_estimate=pl.CostEstimate(
            flops=2 * blocks * scen * panels * panels,
            bytes_accessed=2 * blocks * panels * panels,
            transcendentals=0,
        ),
    )(potentials, injected, near, cols.reshape(rows), rowb, colb, ranks, coup, inv)


def solution(mesh):
    return jax.shard_map(
        functools.partial(local, mesh.shape["prod"], mesh.shape["pre"]),
        mesh=mesh,
        in_specs=(
            P(("prod", "pre"), None, None),
            P(("prod", "pre"), None, None),
            P("prod", "pre", None, None),
            P("prod", "pre"),
            P("prod", None, None),
            P(("prod", "pre"), None, None),
            P(("prod", "pre")),
            P("prod", None, "pre"),
            P(("prod", "pre"), None, None),
        ),
        out_specs=(P(("prod", "pre"), None, None), P(("prod", "pre"), None, None)),
        check_vma=False,
    )
```

time: 81.7 us -> 27.3 us (0.33)
  blocking collectives: 28.3 us -> 0 us
  Pallas kernels: 0 us -> 23.4 us
  waiting for transfers between devices: 20.4 us -> 0 us
  between operations: 14.1 us -> 0.64 us
  matrix products: 10.9 us -> 0 us
  other arithmetic: 3.29 us -> 0 us
  starting transfers between devices: 3.27 us -> 0 us
  local copies, waits for them, and re-layouts: 0.96 us -> 3.14 us
    all_gather x2 -> x0, blocking collectives: 28.3 us -> none  [the longest x1 16 us: local(): grouped = lax.all_gather(potentials, 'pre', axis=0, tiled=True)]
    pallas_call x0 -> x1, Pallas kernels: none -> 23.4 us  [local(): pl.pallas_call(functools.partial(kernel, n_prod, n_pre), out_shape=(out,...]
    reduce_scatter x1 -> x0, waiting for transfers between devices: 20.4 us -> none  [local(): lax.psum_scatter(partial_value.astype(jnp.bfloat16), 'pre', scatter_dimen...]
    dot_general x5 -> x0, matrix products: 10.9 us -> none  [the longest x1 6.38 us: local(): lax.dot_general(picked, near_blocks, (((1, 3), (1, 3)), ((0,), (0,))), pr...]
    ppermute x2 -> x0, starting transfers between devices: 3.23 us -> none  [the longest x1 1.95 us: with_halo(): lax.ppermute(lax.slice_in_dim(block, block.shape[dim] - width, None, axis...]
    unnamed x7 -> x2, local copies, waits for them, and re-layouts: 0.12 us -> 3.14 us
    concatenate x1 -> x0, other arithmetic: 1.03 us -> none  [with_halo(): block = jnp.concatenate([low, block, high], axis=dim)]
    sub x1 -> x0, other arithmetic: 0.85 us -> none  [local(): residual = injected - summed]
  transfers between devices with their start and end apart: 3 -> 0, of which waited for: 1 -> 0; matrix products, arithmetic and copies ran while one was open for 6% -> 0% of each run, Pallas kernels for 0% -> 0%
where the time goes in v1:
time: 27.3 us; the launch traced here: 27.2 us
  Pallas kernels  23.4 us (86%)
  local copies, waits for them, and re-layouts  3.14 us (12%)
  between operations  0.64 us (2%)
    pallas_call x1, Pallas kernels, local(): pl.pallas_call(functools.partial(kernel, n_prod, n_pre), out_shape=(out,...  23.4 us
    unnamed x2, local copies, waits for them, and re-layouts  3.14 us

profile of v1, /device:TPU:0, one launch (start us, length us, event | category | flops | bytes accessed | tf_op | source)
XLA Modules:
  0.0 27.2 jit_solution(3125338290560548303)
XLA Ops:
  0.6 23.4 %shard_map.104 = (f32[4,16,512]{2,1,0:T(8,128)}, f32[4,16,512]{2,1,0:T(8,128)}) custom-call(bf16[4,16,512]{2,1,0:T(8,128)(2,1)} %pot_hbm.1, f32[4,16,512]{2,1,0:T(8,128)} %inj_hbm.1, bf16[16,1,512,512]{3,2,1,0:T(8,128)(2,1)} %near_hbm.1, s32[16]{0:T(128)} %bitcast.1, bf16[16,16,512]{2,1,0:T(8,128)(2,1)} %rowb_hbm.1, bf16[4,16,512]{2,1,0:T(8,128)(2,1)} %colb_hbm.1, ...), custom_call_target="tpu_custom_call" | custom-call | flops 167772160 | bytes 10485760 | tf_op jit(solution)/shard_map/pallas_call | solution.py:299
  24.0 1.6 %copy.13 = f32[4,16,512]{2,1,0:T(8,128)} copy(f32[4,16,512]{2,1,0:T(8,128)} %get-tuple-element.4) | data formatting | bytes 262144
  25.6 1.6 %copy.14 = f32[4,16,512]{2,1,0:T(8,128)} copy(f32[4,16,512]{2,1,0:T(8,128)} %get-tuple-element.5) | data formatting | bytes 262144
